TPU v7x, 32 devices: a whole 2x2x4 slice. The times are simulated.
32 devices in a mesh: design: 2 (over x), gx: 4 (over y, core), gy: 4 (over z).
Axes of the slice: x: 2, y: 2, z: 4, core: 2. Of those that a mesh axis runs over, the one named last changes fastest.
Arguments:
- e_field: float32 [6, 16, 64, 512], P('design', None, 'gx', 'gy'), parts along dimension 0, may hold values from -6 to 6
- h_field: float32 [6, 16, 64, 512], P('design', None, 'gx', 'gy'), parts along dimension 0, may hold values from -6 to 6
- inverse_permittivity: float32 [32, 64, 512], P('design', 'gx', 'gy'), parts along dimension 0, may hold values from 0.0833 to 1
- monitor_layer: int32 [128, 512], P(('design', 'gx'), 'gy'), parts along dimension 0, may hold values from 0 to 15
- source_layer: int32 [128, 512], P(('design', 'gx'), 'gy'), parts along dimension 0, may hold values from 0 to 15
- residual_far: float32 [4, 2, 2, 256, 256], P('design', None, None, 'gx', 'gy'), parts along dimension 0, may hold values from -6 to 6
Outputs:
- e_forward: float32 [6, 16, 64, 512], P('design', None, 'gx', 'gy'), parts along dimension 0
- far_field: float32 [4, 2, 2, 256, 256], P('design', None, None, 'gx', 'gy'), parts along dimension 0
- e_adjoint: float32 [6, 16, 64, 512], P('design', None, 'gx', 'gy'), parts along dimension 0
There are 2 independent parts, one for each index of `design`. A program takes and returns all parts, laid end to end along the dimension named above; each array names one. Nothing has to cross between parts.
All inputs are finite; a program needn't handle non-finite values.
Results may differ from a plain program's by a relative error of at most 0.0001.
Values sent between devices are 32-bit elements; how exact they have to be, the bound alone decides.
A program may use at most 64 MiB of HBM per device.

v0:
```python
import functools
import math

import jax
import jax.numpy as jnp
import numpy as np
from jax import lax
from jax.experimental import pallas as pl
from jax.experimental.pallas import tpu as pltpu
from jax.sharding import PartitionSpec as P

courant = 0.5
omegas = (0.7, 1.3)
factors = (3, 5)
MESH = pl.DeviceIdType.MESH
ticks = (1, 2)


def angles(dirs, length):
    rows = np.arange(dirs)[:, None] - dirs // 2
    cols = np.arange(length)[None, :]
    return np.stack(
        [np.mod(rows * cols * factor, 4 * length) * (2.0 * np.pi / (4 * length)) for factor in factors]
    )


def tables(gx, gy, na, nb, nx, ny):
    theta = angles(gx * na, gx * nx)
    phi = angles(gy * nb, gy * ny)
    freqs = len(factors)
    shifted = np.stack([phi + np.array(omegas)[:, None, None] * t for t in ticks])
    both = np.stack([np.cos(shifted), -np.sin(shifted)], axis=2)
    both = both.reshape(len(ticks), freqs, 2, gy, nb, gy, ny)
    far_y = both.transpose(3, 0, 5, 6, 1, 2, 4).reshape(gy, len(ticks), gy, ny, freqs * 2 * nb)
    back_y = both.transpose(5, 3, 1, 2, 4, 0, 6).reshape(gy, gy, freqs, 2 * nb, len(ticks) * ny)
    back_y = back_y / (gx * na)
    pair = np.stack([np.cos(theta), np.sin(theta)], axis=1).reshape(freqs, 2, gx, na, gx * nx)
    far_x = pair.transpose(2, 0, 1, 3, 4).reshape(gx, freqs, 2 * na, gx * nx)
    far_x = far_x / math.sqrt(gx * nx * gy * ny)
    cos, sin = np.cos(theta), np.sin(theta)
    mix = np.stack([np.stack([cos, -sin]), np.stack([sin, cos])])
    mix = mix.reshape(2, 2, freqs, gx, na, gx, nx)
    back_x = mix.transpose(3, 2, 5, 0, 6, 1, 4).reshape(gx, freqs, gx * 2 * nx, 2 * na)
    return [table.astype(np.float32) for table in (far_y, back_y, far_x, back_x)]


def split(value):
    high = value.astype(jnp.bfloat16)
    return high, (value - high.astype(jnp.float32)).astype(jnp.bfloat16)


def mul(left, right):
    return jnp.dot(left, right, preferred_element_type=jnp.float32)


def triple(left, right):
    return mul(left[0], right[0]) + (mul(left[0], right[1]) + mul(left[1], right[0]))


def kernel(
    gx, gy,
    e_in, h_in, k_in, mon_in, src_in, res_in, far_y_in, back_y_in, far_x_in, back_x_in,
    e_out, far_out, adj_out,
    elec, magn, inv, mon, src, res, far_y32, back_y32, far_x, back_x, far_y, back_y,
    aelec, amagn, afinal, far,
    row_send, col_send, row_recv, col_recv,
    vsend, vrecv, vall, planes, qall,
    in_sems, out_sems, halo_send, halo_recv, v_send, v_recv, g_send, g_recv, p_send, p_recv, q_send, q_recv,
):
    mx = lax.axis_index("gx")
    my = lax.axis_index("gy")
    _, nz, nx, ny = e_in.shape
    na, nb = res_in.shape[3:]
    freqs = len(factors)

    loads = {}
    for slot, (name, source, target) in enumerate((
        ("res", res_in, res),
        ("back_x", back_x_in.at[mx], back_x),
        ("e", e_in, elec.at[:, pl.ds(0, nz)]),
        ("h", h_in, magn.at[:, pl.ds(1, nz)]),
        ("k", k_in, inv),
        ("mon", mon_in, mon),
        ("src", src_in, src),
        ("back_y", back_y_in.at[my], back_y32),
        ("far_y", far_y_in.at[my], far_y32),
        ("far_x", far_x_in.at[mx], far_x),
    )):
        loads[name] = pltpu.make_async_copy(source, target, in_sems.at[slot])
        loads[name].start()

    row_recv[...] = jnp.zeros_like(row_recv)
    col_recv[...] = jnp.zeros_like(col_recv)
    blank = jnp.zeros((nx, ny), jnp.float32)
    for part in range(3):
        elec[part, nz] = blank
        magn[part, 0] = blank
        amagn[part, 0] = blank
    for part in range(2):
        aelec[part, nz] = blank

    barrier = pltpu.get_barrier_semaphore()
    for step in range(1, gx):
        pl.semaphore_signal(barrier, inc=1, device_id={"gx": lax.rem(mx + step, gx)}, device_id_type=MESH)
    for step in range(1, gy):
        pl.semaphore_signal(barrier, inc=1, device_id={"gy": lax.rem(my + step, gy)}, device_id_type=MESH)

    lanes = lax.broadcasted_iota(jnp.int32, (nx, ny), 1)
    rows = lax.broadcasted_iota(jnp.int32, (nx, ny), 0)

    def each_z(body, init):
        return lax.fori_loop(0, nz, body, init, unroll=True)

    def ahead_x(value, edge):
        return jnp.where(rows == nx - 1, edge, pltpu.roll(value, nx - 1, axis=0))

    def behind_x(value, edge):
        return jnp.where(rows == 0, edge, pltpu.roll(value, 1, axis=0))

    def ahead_y(value, packed, lane):
        edge = pltpu.roll(packed, lax.rem(2 * ny - 1 - lane, ny), axis=1)
        return jnp.where(lanes == ny - 1, edge, pltpu.roll(value, ny - 1, axis=1))

    def behind_y(value, packed, lane):
        edge = pltpu.roll(packed, lax.rem(2 * ny - lane, ny), axis=1)
        return jnp.where(lanes == 0, edge, pltpu.roll(value, 1, axis=1))

    def pack_first(value, lane, packed):
        return jnp.where(lanes == lane, pltpu.roll(value, lane, axis=1), packed)

    def pack_last(value, lane, packed):
        return jnp.where(lanes == lane, pltpu.roll(value, lane + 1, axis=1), packed)

    def halo(number, direction, count):
        size = gx, gy
        place = mx, my
        out = []
        for which, (axis, send, recv) in enumerate((("gx", row_send, row_recv), ("gy", col_send, col_recv))):
            here, total = place[which], size[which]
            target = lax.rem(here + direction + total, total)
            source_ref = send.at[number, pl.ds(0, count)] if which == 0 else send.at[number]
            target_ref = recv.at[number, pl.ds(0, count)] if which == 0 else recv.at[number]
            copy = pltpu.make_async_remote_copy(
                src_ref=source_ref,
                dst_ref=target_ref,
                send_sem=halo_send.at[number, which],
                recv_sem=halo_recv.at[number, which],
                device_id={axis: target},
                device_id_type=MESH,
            )
            sends = here >= 1 if direction < 0 else here < total - 1
            takes = here < total - 1 if direction < 0 else here >= 1
            out.append((copy, sends, takes))
        return out

    halos = [halo(number, direction, count) for number, (direction, count) in enumerate(
        ((-1, 2), (1, 2), (-1, 2), (1, 2), (-1, 1), (1, 2)))]

    def send_halo(number):
        for copy, sends, _ in halos[number]:
            pl.when(sends)(copy.start)

    def take_halo(number):
        for copy, _, takes in halos[number]:
            pl.when(takes)(copy.wait_recv)

    def end_halo(number):
        for copy, sends, _ in halos[number]:
            pl.when(sends)(copy.wait_send)

    def spread(axis, source, target, send, recv):
        here, total = (mx, gx) if axis == "gx" else (my, gy)
        out = []
        for step in range(1, total):
            other = lax.rem(here + step, total)
            out.append((
                pltpu.make_async_remote_copy(
                    src_ref=source(other), dst_ref=target(here),
                    send_sem=send(other), recv_sem=recv(here),
                    device_id={axis: other}, device_id_type=MESH),
                pltpu.make_async_remote_copy(
                    src_ref=source(other), dst_ref=target(other),
                    send_sem=send(other), recv_sem=recv(other),
                    device_id={axis: other}, device_id_type=MESH),
            ))
        return out

    def start(copies):
        for copy, _ in copies:
            copy.start()

    def arrive(copies):
        for _, copy in copies:
            copy.wait_recv()

    def left(copies):
        for copy, _ in copies:
            copy.wait_send()

    loads["res"].wait()
    loads["back_x"].wait()
    for f in range(freqs):
        block = jnp.concatenate(
            [jnp.concatenate([res[f, c, 0], res[f, c, 1]], axis=0) for c in range(2)], axis=1)
        part = triple(split(back_x[f]), split(block))
        for other in range(gx):
            vsend[other, f] = part[other * 2 * nx:(other + 1) * 2 * nx]

    loads["e"].wait()

    def pack_start(z, packed):
        row_send[0, 0, pl.ds(z, 1)] = elec[1, z, 0:1]
        row_send[0, 1, pl.ds(z, 1)] = elec[2, z, 0:1]
        packed = pack_first(elec[0, z], z, packed)
        return pack_first(elec[2, z], nz + z, packed)

    col_send[0] = each_z(pack_start, blank)
    pl.semaphore_wait(barrier, gx - 1 + gy - 1)
    send_halo(0)
    v_copies = spread("gx", lambda other: vsend.at[other], lambda slot: vrecv.at[slot],
                      lambda other: v_send.at[other], lambda slot: v_recv.at[slot])
    start(v_copies)

    loads["back_y"].wait()
    for slot in range(gy):
        for f in range(freqs):
            back_y[slot, f, 0], back_y[slot, f, 1] = split(back_y32[slot, f])
    loads["far_y"].wait()
    for tick in range(len(ticks)):
        for slot in range(gy):
            far_y[tick, slot, 0], far_y[tick, slot, 1] = split(far_y32[tick, slot])

    def magnetic(number, after):
        def body(z, packed):
            ex, ey, ez = elec[0, z], elec[1, z], elec[2, z]
            x_face = row_recv.at[number]
            next_x1 = ahead_x(ey, x_face[0, pl.ds(z, 1)])
            next_x2 = ahead_x(ez, x_face[1, pl.ds(z, 1)])
            cols = col_recv[number]
            next_y0 = ahead_y(ex, cols, z)
            next_y2 = ahead_y(ez, cols, nz + z)
            hx = magn[0, z + 1] - courant * ((next_y2 - ez) - (elec[1, z + 1] - ey))
            hy = magn[1, z + 1] - courant * ((elec[0, z + 1] - ex) - (next_x2 - ez))
            hz = magn[2, z + 1] - courant * ((next_x1 - ey) - (next_y0 - ex))
            magn[0, z + 1] = hx
            magn[1, z + 1] = hy
            magn[2, z + 1] = hz
            row_send[after, 0, pl.ds(z, 1)] = hy[nx - 1:nx]
            row_send[after, 1, pl.ds(z, 1)] = hz[nx - 1:nx]
            return pack_last(hz, nz + z, pack_last(hx, z, packed))
        col_send[after] = each_z(body, blank)

    def curls(field, number, z):
        hx, hy, hz = field[0, z + 1], field[1, z + 1], field[2, z + 1]
        x_face = row_recv.at[number]
        prev_x1 = behind_x(hy, x_face[0, pl.ds(z, 1)])
        prev_x2 = behind_x(hz, x_face[1, pl.ds(z, 1)])
        cols = col_recv[number]
        prev_y0 = behind_y(hx, cols, z)
        prev_y2 = behind_y(hz, cols, nz + z)
        curl_x = (hz - prev_y2) - (hy - field[1, z])
        curl_y = (hx - field[0, z]) - (hz - prev_x2)
        curl_z = (hy - prev_x1) - (hx - prev_y0)
        return curl_x, curl_y, curl_z

    def electric(number, after, tick):
        def body(z, carry):
            packed, plane_x, plane_y = carry
            gain = courant * inv[z]
            curl_x, curl_y, curl_z = curls(magn, number, z)
            ex = elec[0, z] + gain * curl_x
            ey = elec[1, z] + gain * curl_y
            ez = elec[2, z] + gain * curl_z
            elec[0, z] = ex
            elec[1, z] = ey
            elec[2, z] = ez
            seen = mon[...] == z
            plane_x = jnp.where(seen, ex, plane_x)
            plane_y = jnp.where(seen, ey, plane_y)
            if after is not None:
                row_send[after, 0, pl.ds(z, 1)] = ey[0:1]
                row_send[after, 1, pl.ds(z, 1)] = ez[0:1]
                packed = pack_first(ez, nz + z, pack_first(ex, z, packed))
            return packed, plane_x, plane_y
        packed, plane_x, plane_y = each_z(body, (blank, blank, blank))
        if after is not None:
            col_send[after] = packed
        planes[tick, my, 0:nx] = plane_x
        planes[tick, my, nx:2 * nx] = plane_y

    def plane_copies(tick):
        return spread("gy", lambda other: planes.at[tick, my], lambda slot: planes.at[tick, slot],
                      lambda other: p_send.at[tick, other], lambda slot: p_recv.at[tick, slot])

    first_planes, second_planes = plane_copies(0), plane_copies(1)
    g_copies = spread("gy", lambda other: vall.at[my], lambda slot: vall.at[slot],
                      lambda other: g_send.at[other], lambda slot: g_recv.at[slot])
    q_copies = spread("gx", lambda other: qall.at[:, mx], lambda slot: qall.at[:, slot],
                      lambda other: q_send.at[other], lambda slot: q_recv.at[slot])

    loads["h"].wait()
    take_halo(0)
    magnetic(0, 1)
    send_halo(1)

    arrive(v_copies)
    vrecv[mx] = vsend[mx]
    for f in range(freqs):
        total = vrecv[0, f]
        for slot in range(1, gx):
            total = total + vrecv[slot, f]
        top, low = total[0:nx], total[nx:2 * nx]
        for c in range(2):
            vall[my, f, c * nx:(c + 1) * nx] = jnp.concatenate(
                [top[:, c * nb:(c + 1) * nb], low[:, c * nb:(c + 1) * nb]], axis=1)
    start(g_copies)

    for name in ("k", "mon", "src"):
        loads[name].wait()
    take_halo(1)
    electric(1, 2, 0)
    send_halo(2)
    start(first_planes)

    take_halo(2)
    magnetic(2, 3)
    send_halo(3)

    arrive(g_copies)
    drive = jnp.zeros((2 * nx, len(ticks) * ny), jnp.float32)
    for slot in range(gy):
        for f in range(freqs):
            drive = drive + triple(split(vall[slot, f]), (back_y[slot, f, 0], back_y[slot, f, 1]))

    def adjoint_first(z, packed):
        lit = jnp.where(src[...] == z, (-courant) * inv[z], 0.0)
        ex = lit * drive[0:nx, 0:ny]
        ey = lit * drive[nx:2 * nx, 0:ny]
        aelec[0, z] = ex
        aelec[1, z] = ey
        row_send[4, 0, pl.ds(z, 1)] = ey[0:1]
        return pack_first(ex, z, packed)

    col_send[4] = each_z(adjoint_first, blank)
    send_halo(4)

    take_halo(3)
    electric(3, None, 1)
    start(second_planes)
    stores = [pltpu.make_async_copy(elec.at[:, pl.ds(0, nz)], e_out, out_sems.at[0])]
    stores[0].start()

    take_halo(4)

    def adjoint_magnetic(z, packed):
        ex, ey = aelec[0, z], aelec[1, z]
        next_x1 = ahead_x(ey, row_recv[4, 0, pl.ds(z, 1)])
        next_y0 = ahead_y(ex, col_recv[4], z)
        hx = courant * (aelec[1, z + 1] - ey)
        hy = (-courant) * (aelec[0, z + 1] - ex)
        hz = (-courant) * ((next_x1 - ey) - (next_y0 - ex))
        amagn[0, z + 1] = hx
        amagn[1, z + 1] = hy
        amagn[2, z + 1] = hz
        row_send[5, 0, pl.ds(z, 1)] = hy[nx - 1:nx]
        row_send[5, 1, pl.ds(z, 1)] = hz[nx - 1:nx]
        return pack_last(hz, nz + z, pack_last(hx, z, packed))

    col_send[5] = each_z(adjoint_magnetic, blank)
    send_halo(5)

    def project(tick):
        total = 0.0
        for slot in range(gy):
            total = total + triple(split(planes[tick, slot]), (far_y[tick, slot, 0], far_y[tick, slot, 1]))
        return total

    arrive(first_planes)
    early = project(0)
    arrive(second_planes)
    half = early + project(1)
    for c in range(2):
        qall[c, mx] = half[c * nx:(c + 1) * nx]
    start(q_copies)

    take_halo(5)

    def adjoint_second(z, carry):
        gain = courant * inv[z]
        curl_x, curl_y, curl_z = curls(amagn, 5, z)
        lit = src[...] == z
        afinal[0, z] = aelec[0, z] + gain * (curl_x - jnp.where(lit, drive[0:nx, ny:2 * ny], 0.0))
        afinal[1, z] = aelec[1, z] + gain * (curl_y - jnp.where(lit, drive[nx:2 * nx, ny:2 * ny], 0.0))
        afinal[2, z] = gain * curl_z
        return carry

    each_z(adjoint_second, 0)
    stores.append(pltpu.make_async_copy(afinal, adj_out, out_sems.at[1]))
    stores[1].start()

    loads["far_x"].wait()
    arrive(q_copies)
    for c in range(2):
        high, low = split(jnp.reshape(qall[c], (gx * nx, freqs * 2 * nb)))
        for f in range(freqs):
            cut = slice(f * 2 * nb, (f + 1) * 2 * nb)
            both = triple(split(far_x[f]), (high[:, cut], low[:, cut]))
            far[f, c, 0] = both[0:na, 0:nb] + both[na:2 * na, nb:2 * nb]
            far[f, c, 1] = both[0:na, nb:2 * nb] - both[na:2 * na, 0:nb]
    stores.append(pltpu.make_async_copy(far, far_out, out_sems.at[2]))
    stores[2].start()

    for number in range(6):
        end_halo(number)
    for copies in (v_copies, g_copies, first_planes, second_planes, q_copies):
        left(copies)
    for copy in stores:
        copy.wait()


def hand_out(e_made, far_made, adj_made, e_out, far_out, adj_out, e_held, far_held, adj_held, load_sems, store_sems):
    moves = []
    for made, held, out in ((e_made, e_held, e_out), (far_made, far_held, far_out), (adj_made, adj_held, adj_out)):
        for part in range(made.shape[0]):
            slot = len(moves)
            moves.append((
                pltpu.make_async_copy(made.at[part], held.at[part], load_sems.at[slot]),
                pltpu.make_async_copy(held.at[part], out.at[part], store_sems.at[slot]),
            ))
    for load, _ in moves:
        load.start()
    for load, store in moves:
        load.wait()
        store.start()
    for _, store in moves:
        store.wait()


def per_device(consts, gx, gy, e_field, h_field, inverse_permittivity, monitor_layer, source_layer, residual_far):
    _, nz, nx, ny = e_field.shape
    freqs = len(factors)
    na, nb = residual_far.shape[3:]
    f32 = jnp.float32
    shapes = [
        pltpu.VMEM((3, nz + 1, nx, ny), f32),
        pltpu.VMEM((3, nz + 1, nx, ny), f32),
        pltpu.VMEM(inverse_permittivity.shape, f32),
        pltpu.VMEM(monitor_layer.shape, jnp.int32),
        pltpu.VMEM(source_layer.shape, jnp.int32),
        pltpu.VMEM(residual_far.shape, f32),
    ] + [pltpu.VMEM(const.shape[1:], f32) for const in consts] + [
        pltpu.VMEM(const.shape[1:-2] + (2,) + const.shape[-2:], jnp.bfloat16) for const in consts[:2]
    ] + [
        pltpu.VMEM((2, nz + 1, nx, ny), f32),
        pltpu.VMEM((3, nz + 1, nx, ny), f32),
        pltpu.VMEM((3, nz, nx, ny), f32),
        pltpu.VMEM(residual_far.shape, f32),
        pltpu.VMEM((6, 2, nz, ny), f32),
        pltpu.VMEM((6, nx, ny), f32),
        pltpu.VMEM((6, 2, nz, ny), f32),
        pltpu.VMEM((6, nx, ny), f32),
        pltpu.VMEM((gx, freqs, 2 * nx, 2 * nb), f32),
        pltpu.VMEM((gx, freqs, 2 * nx, 2 * nb), f32),
        pltpu.VMEM((gy, freqs, 2 * nx, 2 * nb), f32),
        pltpu.VMEM((len(ticks), gy, 2 * nx, ny), f32),
        pltpu.VMEM((2, gx, nx, freqs * 2 * nb), f32),
    ]
    dma = pltpu.SemaphoreType.DMA
    shapes += [dma((10,)), dma((3,)), dma((6, 2)), dma((6, 2)), dma((gx,)), dma((gx,)), dma((gy,)), dma((gy,)),
               dma((len(ticks), gy)), dma((len(ticks), gy)), dma((gx,)), dma((gx,))]
    anywhere = pl.BlockSpec(memory_space=pl.ANY)
    main = pl.BlockSpec(memory_space=pltpu.HBM)
    out_shape = (
        jax.ShapeDtypeStruct(e_field.shape, f32),
        jax.ShapeDtypeStruct(residual_far.shape, f32),
        jax.ShapeDtypeStruct(e_field.shape, f32),
    )
    results = pl.pallas_call(
        functools.partial(kernel, gx, gy),
        out_shape=out_shape,
        in_specs=[main] * 10,
        out_specs=(anywhere,) * 3,
        scratch_shapes=shapes,
        compiler_params=pltpu.CompilerParams(
            collective_id=0, has_side_effects=True, vmem_limit_bytes=64 * 1024 * 1024
        ),
    )(e_field, h_field, inverse_permittivity, monitor_layer, source_layer, residual_far, *consts)
    return pl.pallas_call(
        hand_out,
        out_shape=out_shape,
        in_specs=[anywhere] * 3,
        out_specs=(main,) * 3,
        scratch_shapes=[pltpu.VMEM(shape.shape, f32) for shape in out_shape] + [dma((3 + freqs + 3,))] * 2,
        compiler_params=pltpu.CompilerParams(vmem_limit_bytes=64 * 1024 * 1024),
    )(*results)


def solution(mesh):
    in_specs = (
        P("design", None, "gx", "gy"),
        P("design", None, "gx", "gy"),
        P("design", "gx", "gy"),
        P(("design", "gx"), "gy"),
        P(("design", "gx"), "gy"),
        P("design", None, None, "gx", "gy"),
    )
    out_specs = (
        P("design", None, "gx", "gy"),
        P("design", None, None, "gx", "gy"),
        P("design", None, "gx", "gy"),
    )
    gx, gy = mesh.shape["gx"], mesh.shape["gy"]

    def local(e_field, h_field, inverse_permittivity, monitor_layer, source_layer, residual_far):
        _, _, nx, ny = e_field.shape
        na, nb = residual_far.shape[3:]
        consts = [jnp.asarray(table) for table in tables(gx, gy, na, nb, nx, ny)]
        return per_device(consts, gx, gy, e_field, h_field, inverse_permittivity, monitor_layer,
                          source_layer, residual_far)

    return jax.shard_map(local, mesh=mesh, in_specs=in_specs, out_specs=out_specs, check_vma=False)
```

profile of v0, /device:TPU:0, one launch (start us, length us, event | category | flops | bytes accessed | tf_op | source)
XLA Modules:
  0.0 28.8 jit_solution(15346642815946730703)
XLA Ops:
  0.6 26.1 %shard_map.121 = (f32[3,16,16,128]{3,2,1,0:T(8,128)}, f32[2,2,2,64,64]{4,3,2,1,0:T(8,128)}, f32[3,16,16,128]{3,2,1,0:T(8,128)}) custom-call(f32[3,16,16,128]{3,2,1,0:T(8,128)} %e_in.1, f32[3,16,16,128]{3,2,1,0:T(8,128)} %h_in.1, f32[16,16,128]{2,1,0:T(8,128)} %k_in.1, s32[16,128]{1,0:T(8,128)} %mon_in.1, s32[16,128]{1,0:T(8,128)} %src_in.1, ...), custom_call_target="tpu_custom_call" | custom-call | tf_op jit(solution)/shard_map/pallas_call | solution.py:478
  26.7 2.1 %shard_map.122 = (f32[3,16,16,128]{3,2,1,0:T(8,128)}, f32[2,2,2,64,64]{4,3,2,1,0:T(8,128)}, f32[3,16,16,128]{3,2,1,0:T(8,128)}) custom-call(f32[3,16,16,128]{3,2,1,0:T(8,128)} %get-tuple-element.6.e_made, f32[2,2,2,64,64]{4,3,2,1,0:T(8,128)} %get-tuple-element.7.far_made, f32[3,16,16,128]{3,2,1,0:T(8,128)} %get-tuple-element.8.adj_made), custom_call_target="tpu_custom_call" | custom-call | tf_op jit(solution)/shard_map/pallas_call | solution.py:488
where the time goes:
time: 28.9 us; the launch traced here: 28.8 us
  Pallas kernels  28.1 us (97%)
  between operations  0.64 us (2%)
    pallas_call x1, Pallas kernels, per_device(): pl.pallas_call(functools.partial(kernel, gx, gy), out_shape=out_shape, in...  26.1 us
    pallas_call x1, Pallas kernels, per_device(): pl.pallas_call(hand_out, out_shape=out_shape, in_specs=[anywhere] * 3, ou...  2.09 us

commit v1 on v0

--- a/solution.py
+++ b/solution.py
@@ -63,7 +63,7 @@
     e_out, far_out, adj_out,
     elec, magn, inv, mon, src, res, far_y32, back_y32, far_x, back_x, far_y, back_y,
     aelec, amagn, afinal, far,
-    row_send, col_send, row_recv, col_recv,
+    row_send, col_send, row_recv, col_recv, back_rows, back_cols, took_rows, took_cols, corner_row, corner_col,
     vsend, vrecv, vall, planes, qall,
     in_sems, out_sems, halo_send, halo_recv, v_send, v_recv, g_send, g_recv, p_send, p_recv, q_send, q_recv,
 ):
@@ -91,6 +91,8 @@
 
     row_recv[...] = jnp.zeros_like(row_recv)
     col_recv[...] = jnp.zeros_like(col_recv)
+    for ref in (took_rows, took_cols, corner_row, corner_col):
+        ref[...] = jnp.zeros_like(ref)
     blank = jnp.zeros((nx, ny), jnp.float32)
     for part in range(3):
         elec[part, nz] = blank
@@ -104,6 +106,14 @@
         pl.semaphore_signal(barrier, inc=1, device_id={"gx": lax.rem(mx + step, gx)}, device_id_type=MESH)
     for step in range(1, gy):
         pl.semaphore_signal(barrier, inc=1, device_id={"gy": lax.rem(my + step, gy)}, device_id_type=MESH)
+
+    has_fore = (mx < gx - 1) & (my >= 1)
+    has_aft = (mx >= 1) & (my < gy - 1)
+    fore = {"gx": lax.rem(mx + 1, gx), "gy": lax.rem(my + gy - 1, gy)}
+    aft = {"gx": lax.rem(mx + gx - 1, gx), "gy": lax.rem(my + 1, gy)}
+
+    for diagonal in (fore, aft):
+        pl.semaphore_signal(barrier, inc=1, device_id=diagonal, device_id_type=MESH)
 
     lanes = lax.broadcasted_iota(jnp.int32, (nx, ny), 1)
     rows = lax.broadcasted_iota(jnp.int32, (nx, ny), 0)
@@ -153,8 +163,25 @@
             out.append((copy, sends, takes))
         return out
 
-    halos = [halo(number, direction, count) for number, (direction, count) in enumerate(
-        ((-1, 2), (1, 2), (-1, 2), (1, 2), (-1, 1), (1, 2)))]
+    def wide(number):
+        step = number // 2
+        out = []
+        for which, source, target, device, sends, takes in (
+            (2, back_rows.at[step], took_rows.at[step], {"gx": lax.rem(mx + 1, gx)}, mx < gx - 1, mx >= 1),
+            (3, back_cols.at[step], took_cols.at[step], {"gy": lax.rem(my + 1, gy)}, my < gy - 1, my >= 1),
+            (4, back_rows.at[step, 2], corner_row.at[step], fore, has_fore, has_aft),
+            (5, back_cols.at[step], corner_col.at[step], aft, has_aft, has_fore),
+        ):
+            out.append((pltpu.make_async_remote_copy(
+                src_ref=source, dst_ref=target,
+                send_sem=halo_send.at[number, which], recv_sem=halo_recv.at[number, which],
+                device_id=device, device_id_type=MESH), sends, takes))
+        return out
+
+    halos = {number: halo(number, direction, count) for number, direction, count in (
+        (0, -1, 2), (2, -1, 2), (4, -1, 1), (5, 1, 2))}
+    for number in (0, 2):
+        halos[number] += wide(number)
 
     def send_halo(number):
         for copy, sends, _ in halos[number]:
@@ -208,14 +235,24 @@
 
     loads["e"].wait()
 
-    def pack_start(z, packed):
-        row_send[0, 0, pl.ds(z, 1)] = elec[1, z, 0:1]
-        row_send[0, 1, pl.ds(z, 1)] = elec[2, z, 0:1]
-        packed = pack_first(elec[0, z], z, packed)
-        return pack_first(elec[2, z], nz + z, packed)
-
-    col_send[0] = each_z(pack_start, blank)
-    pl.semaphore_wait(barrier, gx - 1 + gy - 1)
+    loads["h"].wait()
+
+    def pack_start(z, carry):
+        first, last = carry
+        ex, ey, ez = elec[0, z], elec[1, z], elec[2, z]
+        hx, hy, hz = magn[0, z + 1], magn[1, z + 1], magn[2, z + 1]
+        row_send[0, 0, pl.ds(z, 1)] = ey[0:1]
+        row_send[0, 1, pl.ds(z, 1)] = ez[0:1]
+        first = pack_first(ez, nz + z, pack_first(ex, z, first))
+        for slot, value in enumerate((hy, hz, ex, ey, ez)):
+            back_rows[0, slot, pl.ds(z, 1)] = value[nx - 1:nx]
+        for slot, value in enumerate((hx, hz, ex, ey, ez)):
+            last = pack_last(value, slot * nz + z, last)
+        return first, last
+
+    col_send[0], back_cols[0] = each_z(pack_start, (blank, blank))
+    pl.semaphore_wait(barrier, gx + gy)
+
     send_halo(0)
     v_copies = spread("gx", lambda other: vsend.at[other], lambda slot: vrecv.at[slot],
                       lambda other: v_send.at[other], lambda slot: v_recv.at[slot])
@@ -230,7 +267,31 @@
         for slot in range(gy):
             far_y[tick, slot, 0], far_y[tick, slot, 1] = split(far_y32[tick, slot])
 
-    def magnetic(number, after):
+    zrows = lax.broadcasted_iota(jnp.int32, (nz, ny), 0)
+
+    def left_by(value, count):
+        return pltpu.roll(value, (2 * ny - count) % ny, axis=1)
+
+    def borders(number):
+        step = number // 2
+        hy, hz, ex, ey, ez = [took_rows[step, slot] for slot in range(5)]
+        up = jnp.where(zrows == nz - 1, 0.0, pltpu.roll(ex, nz - 1, axis=0))
+        hy = hy - courant * ((up - ex) - (row_send[number, 1] - ez))
+        side = jnp.where(jnp.broadcast_to(lanes[0:1], (nz, ny)) == ny - 1,
+                         pltpu.roll(corner_row[step], ny - 1, axis=1), pltpu.roll(ex, ny - 1, axis=1))
+        hz = hz - courant * ((row_send[number, 0] - ey) - (side - ex))
+        row_recv[number + 1, 0] = jnp.where(mx >= 1, hy, 0.0)
+        row_recv[number + 1, 1] = jnp.where(mx >= 1, hz, 0.0)
+        took, mine = took_cols[step], col_send[number]
+        ey = left_by(took, 3 * nz)
+        up = jnp.where(lanes == nz - 1, 0.0, left_by(took, 3 * nz + 1))
+        hx = took - courant * ((left_by(mine, nz) - left_by(took, 4 * nz)) - (up - ey))
+        side = ahead_x(took, pltpu.roll(corner_col[step], nx - 1, axis=0))
+        hz = took - courant * ((left_by(side, 2 * nz) - left_by(took, 2 * nz))
+                               - (left_by(mine, ny - nz) - left_by(took, nz)))
+        col_recv[number + 1] = jnp.where(my >= 1, jnp.where(lanes < nz, hx, hz), 0.0)
+
+    def magnetic(number, wider):
         def body(z, packed):
             ex, ey, ez = elec[0, z], elec[1, z], elec[2, z]
             x_face = row_recv.at[number]
@@ -245,10 +306,14 @@
             magn[0, z + 1] = hx
             magn[1, z + 1] = hy
             magn[2, z + 1] = hz
-            row_send[after, 0, pl.ds(z, 1)] = hy[nx - 1:nx]
-            row_send[after, 1, pl.ds(z, 1)] = hz[nx - 1:nx]
-            return pack_last(hz, nz + z, pack_last(hx, z, packed))
-        col_send[after] = each_z(body, blank)
+            if wider:
+                back_rows[1, 0, pl.ds(z, 1)] = hy[nx - 1:nx]
+                back_rows[1, 1, pl.ds(z, 1)] = hz[nx - 1:nx]
+                packed = pack_last(hz, nz + z, pack_last(hx, z, packed))
+            return packed
+        packed = each_z(body, blank)
+        if wider:
+            back_cols[1] = packed
 
     def curls(field, number, z):
         hx, hy, hz = field[0, z + 1], field[1, z + 1], field[2, z + 1]
@@ -265,7 +330,7 @@
 
     def electric(number, after, tick):
         def body(z, carry):
-            packed, plane_x, plane_y = carry
+            packed, last, plane_x, plane_y = carry
             gain = courant * inv[z]
             curl_x, curl_y, curl_z = curls(magn, number, z)
             ex = elec[0, z] + gain * curl_x
@@ -281,10 +346,14 @@
                 row_send[after, 0, pl.ds(z, 1)] = ey[0:1]
                 row_send[after, 1, pl.ds(z, 1)] = ez[0:1]
                 packed = pack_first(ez, nz + z, pack_first(ex, z, packed))
-            return packed, plane_x, plane_y
-        packed, plane_x, plane_y = each_z(body, (blank, blank, blank))
+                for slot, value in ((2, ex), (3, ey), (4, ez)):
+                    back_rows[1, slot, pl.ds(z, 1)] = value[nx - 1:nx]
+                    last = pack_last(value, slot * nz + z, last)
+            return packed, last, plane_x, plane_y
+        packed, last, plane_x, plane_y = each_z(body, (blank, back_cols[1], blank, blank))
         if after is not None:
             col_send[after] = packed
+            back_cols[1] = last
         planes[tick, my, 0:nx] = plane_x
         planes[tick, my, nx:2 * nx] = plane_y
 
@@ -298,10 +367,8 @@
     q_copies = spread("gx", lambda other: qall.at[:, mx], lambda slot: qall.at[:, slot],
                       lambda other: q_send.at[other], lambda slot: q_recv.at[slot])
 
-    loads["h"].wait()
     take_halo(0)
-    magnetic(0, 1)
-    send_halo(1)
+    borders(0)
 
     arrive(v_copies)
     vrecv[mx] = vsend[mx]
@@ -317,14 +384,10 @@
 
     for name in ("k", "mon", "src"):
         loads[name].wait()
-    take_halo(1)
+    magnetic(0, True)
     electric(1, 2, 0)
     send_halo(2)
     start(first_planes)
-
-    take_halo(2)
-    magnetic(2, 3)
-    send_halo(3)
 
     arrive(g_copies)
     drive = jnp.zeros((2 * nx, len(ticks) * ny), jnp.float32)
@@ -344,7 +407,9 @@
     col_send[4] = each_z(adjoint_first, blank)
     send_halo(4)
 
-    take_halo(3)
+    take_halo(2)
+    borders(2)
+    magnetic(2, False)
     electric(3, None, 1)
     start(second_planes)
     stores = [pltpu.make_async_copy(elec.at[:, pl.ds(0, nz)], e_out, out_sems.at[0])]
@@ -410,7 +475,7 @@
     stores.append(pltpu.make_async_copy(far, far_out, out_sems.at[2]))
     stores[2].start()
 
-    for number in range(6):
+    for number in (0, 2, 4, 5):
         end_halo(number)
     for copies in (v_copies, g_copies, first_planes, second_planes, q_copies):
         left(copies)
@@ -459,6 +524,12 @@
         pltpu.VMEM((6, nx, ny), f32),
         pltpu.VMEM((6, 2, nz, ny), f32),
         pltpu.VMEM((6, nx, ny), f32),
+        pltpu.VMEM((2, 5, nz, ny), f32),
+        pltpu.VMEM((2, nx, ny), f32),
+        pltpu.VMEM((2, 5, nz, ny), f32),
+        pltpu.VMEM((2, nx, ny), f32),
+        pltpu.VMEM((2, nz, ny), f32),
+        pltpu.VMEM((2, nx, ny), f32),
         pltpu.VMEM((gx, freqs, 2 * nx, 2 * nb), f32),
         pltpu.VMEM((gx, freqs, 2 * nx, 2 * nb), f32),
         pltpu.VMEM((gy, freqs, 2 * nx, 2 * nb), f32),
@@ -466,7 +537,7 @@
         pltpu.VMEM((2, gx, nx, freqs * 2 * nb), f32),
     ]
     dma = pltpu.SemaphoreType.DMA
-    shapes += [dma((10,)), dma((3,)), dma((6, 2)), dma((6, 2)), dma((gx,)), dma((gx,)), dma((gy,)), dma((gy,)),
+    shapes += [dma((10,)), dma((3,)), dma((6, 6)), dma((6, 6)), dma((gx,)), dma((gx,)), dma((gy,)), dma((gy,)),
                dma((len(ticks), gy)), dma((len(ticks), gy)), dma((gx,)), dma((gx,))]
     anywhere = pl.BlockSpec(memory_space=pl.ANY)
     main = pl.BlockSpec(memory_space=pltpu.HBM)

time: 28.9 us -> 27.3 us (0.945)
  Pallas kernels: 28.1 us -> 26.5 us
    pallas_call x1, Pallas kernels: 26.1 us -> 24.5 us  [per_device(): pl.pallas_call(functools.partial(kernel, gx, gy), out_shape=out_shape, in...]
where the time goes in v1:
time: 27.3 us; the launch traced here: 27.2 us
  Pallas kernels  26.5 us (97%)
  between operations  0.64 us (2%)
    pallas_call x1, Pallas kernels, per_device(): pl.pallas_call(functools.partial(kernel, gx, gy), out_shape=out_shape, in...  24.5 us
    pallas_call x1, Pallas kernels, per_device(): pl.pallas_call(hand_out, out_shape=out_shape, in_specs=[anywhere] * 3, ou...  2.09 us

profile of v1, /device:TPU:0, one launch (start us, length us, event | category | flops | bytes accessed | tf_op | source)
XLA Modules:
  0.0 27.2 jit_solution(5233306409840383423)
XLA Ops:
  0.6 24.5 %shard_map.121 = (f32[3,16,16,128]{3,2,1,0:T(8,128)}, f32[2,2,2,64,64]{4,3,2,1,0:T(8,128)}, f32[3,16,16,128]{3,2,1,0:T(8,128)}) custom-call(f32[3,16,16,128]{3,2,1,0:T(8,128)} %e_in.1, f32[3,16,16,128]{3,2,1,0:T(8,128)} %h_in.1, f32[16,16,128]{2,1,0:T(8,128)} %k_in.1, s32[16,128]{1,0:T(8,128)} %mon_in.1, s32[16,128]{1,0:T(8,128)} %src_in.1, ...), custom_call_target="tpu_custom_call" | custom-call | tf_op jit(solution)/shard_map/pallas_call | solution.py:549
  25.1 2.1 %shard_map.122 = (f32[3,16,16,128]{3,2,1,0:T(8,128)}, f32[2,2,2,64,64]{4,3,2,1,0:T(8,128)}, f32[3,16,16,128]{3,2,1,0:T(8,128)}) custom-call(f32[3,16,16,128]{3,2,1,0:T(8,128)} %get-tuple-element.6.e_made, f32[2,2,2,64,64]{4,3,2,1,0:T(8,128)} %get-tuple-element.7.far_made, f32[3,16,16,128]{3,2,1,0:T(8,128)} %get-tuple-element.8.adj_made), custom_call_target="tpu_custom_call" | custom-call | tf_op jit(solution)/shard_map/pallas_call | solution.py:559

commit v2 on v1

--- a/solution.py
+++ b/solution.py
@@ -75,10 +75,10 @@
 
     loads = {}
     for slot, (name, source, target) in enumerate((
+        ("e", e_in, elec.at[:, pl.ds(0, nz)]),
+        ("h", h_in, magn.at[:, pl.ds(1, nz)]),
         ("res", res_in, res),
         ("back_x", back_x_in.at[mx], back_x),
-        ("e", e_in, elec.at[:, pl.ds(0, nz)]),
-        ("h", h_in, magn.at[:, pl.ds(1, nz)]),
         ("k", k_in, inv),
         ("mon", mon_in, mon),
         ("src", src_in, src),
@@ -224,15 +224,6 @@
         for copy, _ in copies:
             copy.wait_send()
 
-    loads["res"].wait()
-    loads["back_x"].wait()
-    for f in range(freqs):
-        block = jnp.concatenate(
-            [jnp.concatenate([res[f, c, 0], res[f, c, 1]], axis=0) for c in range(2)], axis=1)
-        part = triple(split(back_x[f]), split(block))
-        for other in range(gx):
-            vsend[other, f] = part[other * 2 * nx:(other + 1) * 2 * nx]
-
     loads["e"].wait()
 
     loads["h"].wait()
@@ -254,6 +245,16 @@
     pl.semaphore_wait(barrier, gx + gy)
 
     send_halo(0)
+
+    loads["res"].wait()
+    loads["back_x"].wait()
+    for f in range(freqs):
+        block = jnp.concatenate(
+            [jnp.concatenate([res[f, c, 0], res[f, c, 1]], axis=0) for c in range(2)], axis=1)
+        part = triple(split(back_x[f]), split(block))
+        for other in range(gx):
+            vsend[other, f] = part[other * 2 * nx:(other + 1) * 2 * nx]
+
     v_copies = spread("gx", lambda other: vsend.at[other], lambda slot: vrecv.at[slot],
                       lambda other: v_send.at[other], lambda slot: v_recv.at[slot])
     start(v_copies)

time: 27.3 us -> 27.6 us (1.011)
  Pallas kernels: 26.5 us -> 26.8 us
where the time goes in v2:
time: 27.6 us; the launch traced here: 27.4 us
  Pallas kernels  26.8 us (97%)
  between operations  0.64 us (2%)
    pallas_call x1, Pallas kernels, per_device(): pl.pallas_call(functools.partial(kernel, gx, gy), out_shape=out_shape, in...  24.7 us
    pallas_call x1, Pallas kernels, per_device(): pl.pallas_call(hand_out, out_shape=out_shape, in_specs=[anywhere] * 3, ou...  2.09 us

profile of v2, /device:TPU:0, one launch (start us, length us, event | category | flops | bytes accessed | tf_op | source)
XLA Modules:
  0.0 27.4 jit_solution(9899611529981427842)
XLA Ops:
  0.6 24.7 %shard_map.121 = (f32[3,16,16,128]{3,2,1,0:T(8,128)}, f32[2,2,2,64,64]{4,3,2,1,0:T(8,128)}, f32[3,16,16,128]{3,2,1,0:T(8,128)}) custom-call(f32[3,16,16,128]{3,2,1,0:T(8,128)} %e_in.1, f32[3,16,16,128]{3,2,1,0:T(8,128)} %h_in.1, f32[16,16,128]{2,1,0:T(8,128)} %k_in.1, s32[16,128]{1,0:T(8,128)} %mon_in.1, s32[16,128]{1,0:T(8,128)} %src_in.1, ...), custom_call_target="tpu_custom_call" | custom-call | tf_op jit(solution)/shard_map/pallas_call | solution.py:550
  25.3 2.1 %shard_map.122 = (f32[3,16,16,128]{3,2,1,0:T(8,128)}, f32[2,2,2,64,64]{4,3,2,1,0:T(8,128)}, f32[3,16,16,128]{3,2,1,0:T(8,128)}) custom-call(f32[3,16,16,128]{3,2,1,0:T(8,128)} %get-tuple-element.6.e_made, f32[2,2,2,64,64]{4,3,2,1,0:T(8,128)} %get-tuple-element.7.far_made, f32[3,16,16,128]{3,2,1,0:T(8,128)} %get-tuple-element.8.adj_made), custom_call_target="tpu_custom_call" | custom-call | tf_op jit(solution)/shard_map/pallas_call | solution.py:560
